TPU v7x, 256 devices: a whole 4x4x8 slice. The times are simulated.
256 devices in a mesh: orb: 8 (over z_lo, y), fft: 32 (over x, z_hi, core).
Axes of the slice: x: 4, y: 4, z: 8 (z_hi: 4, z_lo: 2; z = z_hi * 2 + z_lo), core: 2. Of those that a mesh axis runs over, the one named last changes fastest.
Arguments:
- targets: float32 [8, 128, 128, 128], P('orb', 'fft'), may hold values from -6 to 6
- occupied: float32 [8, 128, 128, 128], P('orb', 'fft'), may hold values from -6 to 6
- sphere_map: int32 [131072], P('fft'), may hold values from 0 to 65535, as said below
Outputs:
- exchange_sphere: float32 [8, 2, 131072], P('orb', None, 'fft')
Inputs may be any that keep to these rules, and one draw needn't show every extreme that they name: `sphere_map`: within each aligned block of 4096 entries the entries are distinct cells of that block's spectral slab, numbered over 128 x 4 x 128 cells in that order; the block holds exactly one cell of every aligned run of 16 cells.
All inputs are finite; a program needn't handle non-finite values.
Results may differ from a plain program's by a relative error of at most 0.0001.
Values sent between devices are 32-bit elements; how exact they have to be, the bound alone decides.
No kernel may reach another device: no remote copies, remote signals or barrier semaphores. Data moves between devices by JAX's collectives and lax.ppermute only.
A program may use at most 128 MiB of HBM per device.

v0:
```python
import functools

import jax
import jax.numpy as jnp
import ml_dtypes
import numpy as np
from jax import lax
from jax.experimental import pallas as pl
from jax.experimental.pallas import tpu as pltpu
from jax.sharding import Mesh
from jax.sharding import PartitionSpec as P

box_length = 82.0
screening = 0.106
grid = 128
axes = ("zlo", "y", "x", "zhi", "core")
extent = {"zlo": 2, "y": 4, "x": 4, "zhi": 4, "core": 2}
vmem = pl.BlockSpec(memory_space=pltpu.VMEM)
smem = pl.BlockSpec(memory_space=pltpu.SMEM)
params = pltpu.CompilerParams(vmem_limit_bytes=16 * 1024 * 1024)


def split_table(table):
    high = table.astype(ml_dtypes.bfloat16)
    low = (table - high.astype(np.float64)).astype(ml_dtypes.bfloat16)
    return high, low


def waves(rows, cols):
    angles = (np.outer(rows, cols) % grid) * (2.0 * np.pi / grid)
    return np.cos(angles), np.sin(angles)


def base_table():
    cosine, sine = waves(np.arange(grid), np.arange(grid))
    return np.stack(split_table(np.block([[cosine, sine], [-sine, cosine]])))


names = ("z", "zi", "y", "yi", "x", "xi", "y_end", "x_end")
steps = tuple((r, c) for r in (2, 1, 3, 0) for c in (0, 1))
returns = (2, 1, 3, 0)
parts = ((0, 3), (3, 1))


def halves(value):
    high = value.astype(jnp.bfloat16)
    low = (value - high.astype(jnp.float32)).astype(jnp.bfloat16)
    return high, low


def product(left, right):
    def one(a, b):
        return lax.dot_general(a, b, (((1,), (0,)), ((), ())), preferred_element_type=jnp.float32)

    return one(left[0], right[0]) + (one(left[0], right[1]) + one(left[1], right[0]))


def read(pair):
    return pair[0], pair[1]


def planes_to_columns(value):
    top = [value[p * grid : (p + 1) * grid, :grid] for p in range(4)]
    low = [value[p * grid : (p + 1) * grid, grid:] for p in range(4)]
    return jnp.concatenate([jnp.concatenate(top, axis=1), jnp.concatenate(low, axis=1)], axis=0)


def columns_to_planes(value):
    parts = []
    for p in range(4):
        block = value[:, p * grid : (p + 1) * grid]
        parts.append(jnp.concatenate([block[:grid], block[grid:]], axis=1))
    return jnp.concatenate(parts, axis=0)


def choose(index, refs):
    value = refs[0][...]
    for at in range(1, len(refs)):
        value = jnp.where(index == at, refs[at][...], value)
    return value


def part(ref, at, rows):
    return ref[pl.ds(at * rows, rows), :]


def table_kernel(place, base, *outs):
    x, core, y, zhi, side = (place[8 + n] for n in range(5))
    at = lax.broadcasted_iota(jnp.int32, (2 * grid, 1), 0)
    goal = lax.broadcasted_iota(jnp.int32, (2 * grid, 2 * grid), 1)

    def pick(index, values):
        out = values[0]
        for n in range(1, len(values)):
            out = jnp.where(index == n, values[n], out)
        return out

    def order(index):
        return (goal == index).astype(jnp.bfloat16)

    step = at >> 5
    far = pick(step >> 1, (2, 1, 3, 0))
    twin = (core + step) & 1

    def block(sign):
        chip = ((x + 4 + sign * far) & 3) * 2 + twin
        return ((at >> 4) & 1) * grid + chip * 16 + (at & 15)

    def planes(sign, piece):
        line = (sign * 32 * far + grid + 8 * piece + 4 * twin + ((at >> 1) & 3)) & (grid - 1)
        return (at & 1) * grid + line

    slot = (at >> 3) & 3
    staged = (zhi + 4 + pick(slot, (0, side, -side, 2))) & 3
    returned = (y + 2 + pick(slot, returns)) & 3
    line = ((at >> 6) & 3) * 32 + (((at >> 4) + 3 + side) & 3) * 8 + ((at >> 3) & 1) * 4
    row_end = ((at >> 2) & 1) * grid + line + (at & 3)
    column_end = (at & 1) * grid + line + ((at >> 1) & 3)

    def turned(left, right):
        product = lax.dot_general(
            left, right, (((1,), (1,)), ((), ())), preferred_element_type=jnp.float32
        )
        return product.astype(jnp.bfloat16)

    same = order(at)
    rows_y, columns_y = order(block(1)), order(block(-1))
    columns_x, rows_x = order(planes(-1, staged)), order(planes(1, returned))
    rows_end, columns_end = order(row_end), order(column_end)
    for half in range(2):
        forward = base[half]
        inverse = turned(same, forward)
        values = (
            inverse,
            forward,
            turned(rows_y, inverse),
            turned(inverse, columns_y),
            turned(forward, columns_x),
            turned(rows_x, forward),
            turned(rows_end, inverse),
            turned(forward, columns_end),
        )
        for out, value in zip(outs, values):
            out[half] = value


def density_kernel(first, count, place, *refs):
    targets, pairs, tables = refs[:4], refs[4 : 4 + 2 * count], refs[4 + 2 * count : 6 + 2 * count]
    kept, outs = refs[6 + 2 * count : -8], refs[-8:]
    z_table, y_table = read(tables[0]), read(tables[1])
    for earlier, out in zip(kept, outs):
        out[pl.ds(0, first * 128), :] = earlier[...]
    for at in range(count):
        band = choose(place[first + at], targets)
        packed = jnp.concatenate([band * pairs[2 * at][...], band * pairs[2 * at + 1][...]], axis=1)
        lines = product(halves(packed), z_table)
        spread = product(y_table, halves(planes_to_columns(lines)))
        for step, out in enumerate(outs):
            for p in range(4):
                out[pl.ds(((first + at) * 4 + p) * 32, 32), :] = spread[
                    step * 32 : (step + 1) * 32, p * grid : (p + 1) * grid
                ]


def convolve_kernel(weights, x_pair, xi_pair, *refs):
    arrived, outs = refs[:8], refs[8:]
    x_table, xi_table = read(x_pair), read(xi_pair)
    for pair in range(8):
        columns = [
            jnp.concatenate([ref[pl.ds(2 * pair + k, 32, 16), :] for ref in arrived], axis=0)
            for k in range(2)
        ]
        spectrum = product(x_table, halves(jnp.concatenate(columns, axis=1)))
        weight = weights[:, pl.ds(pair * 2 * grid, 2 * grid)]
        scaled = jnp.concatenate([spectrum[:grid] * weight, spectrum[grid:] * weight], axis=0)
        back = product(xi_table, halves(scaled))
        for k in range(2):
            for at, out in enumerate(outs):
                out[pl.ds(2 * pair + k, 32, 16), :] = back[
                    at * 32 : (at + 1) * 32, k * grid : (k + 1) * grid
                ]


def field_kernel(first, place, *refs):
    arrived, owns, others = refs[:8], refs[8:12], refs[12:16]
    yi_table, zi_table, outs = read(refs[16]), read(refs[17]), refs[18:]
    for at, out in enumerate(outs):
        rows = jnp.concatenate(
            [
                jnp.concatenate([part(ref, (first + at) * 4 + p, 32) for ref in arrived], axis=0)
                for p in range(4)
            ],
            axis=1,
        )
        lines = product(yi_table, halves(rows))
        values = product(halves(columns_to_planes(lines)), zi_table)
        own, other = choose(place[4 + first + at], owns), choose(place[4 + first + at], others)
        out[...] = -(own * values[:, :grid] + other * values[:, grid:])


def applied_kernel(own, one, two, three, z_pair, y_pair, out):
    applied = (own[...] + one[...]) + (two[...] + three[...])
    lines = product(halves(applied), (z_pair[0, :grid], z_pair[1, :grid]))
    spread = product(read(y_pair), halves(planes_to_columns(lines)))
    for p in range(4):
        out[:, pl.ds(p, 1)] = spread[:, p * grid : (p + 1) * grid].reshape(32, 1, 8, grid)


def mask_kernel(cells, out, plane_out, run_out):
    cell = cells[...]

    def hot(count, index):
        return lax.broadcasted_iota(jnp.int32, (count, 4096), 0) == index

    row_hot = hot(512, cell // grid).astype(jnp.bfloat16)
    lane_hot = hot(grid, cell % grid).astype(jnp.bfloat16)
    out[...] = lax.dot_general(
        row_hot, lane_hot, (((1,), (1,)), ((), ())), preferred_element_type=jnp.float32
    )
    plane_out[...] = hot(grid, cell // 512).astype(jnp.bfloat16)
    run_out[...] = hot(32, (cell // 16) % 32).astype(jnp.float32)


def pick_kernel(arrived, mask, planes, runs_at, x_pair, out):
    x_table = read(x_pair)
    lane = lax.broadcasted_iota(jnp.int32, (grid, grid), 0)
    group = lax.broadcasted_iota(jnp.int32, (grid, grid), 1)
    total = jnp.zeros((2 * grid, grid), jnp.float32)
    for pair in range(2):
        columns = [arrived[pl.ds(2 * pair + k, 2 * grid, 4), :] for k in range(2)]
        spectrum = product(x_table, halves(jnp.concatenate(columns, axis=1)))
        for k in range(2):
            row = 2 * pair + k
            kept = mask[pl.ds(row, grid, 4), :]
            part = spectrum[:, k * grid : (k + 1) * grid]
            part = jnp.concatenate([part[:grid] * kept, part[grid:] * kept], axis=0)
            ones = (group == row * 8 + lane // 16).astype(jnp.bfloat16)
            for piece in halves(part):
                total = total + lax.dot_general(
                    piece, ones, (((1,), (0,)), ((), ())), preferred_element_type=jnp.float32
                )
    norm = 1.0 / float(np.sqrt(float(grid) ** 3))
    for c in range(2):
        runs = total[c * grid : (c + 1) * grid].T[:32]
        spread = jnp.zeros((32, 4096), jnp.float32)
        for piece in halves(runs):
            spread = spread + lax.dot_general(
                piece, planes[...], (((1,), (0,)), ((), ())), preferred_element_type=jnp.float32
            )
        out[pl.ds(c, 1), :] = (
            jnp.sum(runs_at[...] * spread, axis=0, keepdims=True) * norm
        )


def call(kernel, shapes, specs, *args, flops=1 << 30):
    return pl.pallas_call(
        kernel,
        out_shape=shapes,
        in_specs=specs,
        out_specs=jax.tree.map(lambda _: vmem, shapes),
        compiler_params=params,
        cost_estimate=pl.CostEstimate(flops=flops, bytes_accessed=1 << 20, transcendentals=0),
    )(*args)


def floats(*shape):
    return jax.ShapeDtypeStruct(shape, jnp.float32)


def moved(change):
    pairs = []
    sizes = tuple(extent[a] for a in axes)
    for at in np.ndindex(sizes):
        spot = dict(zip(axes, at))
        goal = change(dict(spot))
        pairs.append((int(np.ravel_multi_index(at, sizes)),
                      int(np.ravel_multi_index(tuple(goal[a] for a in axes), sizes))))
    return pairs


def swapped(spot):
    turn = 2 * spot["zlo"]
    spot["y"], spot["zhi"] = (spot["zhi"] + 2 + turn) % 4, (spot["y"] + turn) % 4
    return spot


def swapped_back(spot):
    turn = 2 * spot["zlo"]
    spot["y"], spot["zhi"] = (spot["zhi"] + turn) % 4, (spot["y"] + 2 + turn) % 4
    return spot


def along_y(step):
    def change(spot):
        spot["y"] = (spot["y"] + step) % 4
        return spot

    return moved(change)


def along_x(step, turn):
    def change(spot):
        spot["x"] = (spot["x"] + step) % 4
        spot["core"] = (spot["core"] + turn) % 2
        return spot

    return moved(change)


def with_partner(spot):
    spot["zlo"] = 1 - spot["zlo"]
    return spot


def with_border(spot):
    z = (spot["zhi"] * 2 + spot["zlo"] + (1 if spot["zlo"] else -1)) % 8
    spot["zhi"], spot["zlo"] = z // 2, z % 2
    return spot


def send(value, pairs):
    return lax.ppermute(value, axes, pairs)


def after(value, *others):
    return lax.optimization_barrier((value,) + others)[0]


def screened_weights(first_row):
    counter = jnp.arange(grid, dtype=jnp.int32)
    folded = jnp.where(counter < grid // 2, counter, counter - grid).astype(jnp.float32)
    rows = first_row + jnp.arange(16, dtype=jnp.int32)
    folded_rows = jnp.where(rows < grid // 2, rows, rows - grid).astype(jnp.float32)
    factor = (2.0 * jnp.pi / box_length) ** 2
    square_norm = factor * (
        folded[:, None, None] ** 2 + folded_rows[None, :, None] ** 2 + folded[None, None, :] ** 2
    )
    safe_square = jnp.where(square_norm > 0, square_norm, 1.0)
    screened = 4.0 * jnp.pi / safe_square * (1.0 - jnp.exp(-safe_square / (4.0 * screening * screening)))
    kernel = jnp.where(square_norm > 0, screened, jnp.pi / (screening * screening))
    return (kernel * (1.0 / grid**3)).reshape(grid, 16 * grid)


def exchange(blocks):
    return [
        block if step == (0, 0) else send(block, along_x(*step)) for step, block in zip(steps, blocks)
    ]


def local(targets, occupied, sphere_map):
    spot = {name: lax.axis_index(name) for name in axes}
    x, y, zhi, zlo, core = (spot[name] for name in ("x", "y", "zhi", "zlo", "core"))
    side = 2 * zlo - 1
    chip = x * 2 + core
    turns = (0, side, -side, 2)
    turned = (y + 2 * zlo) % 4
    band_at = [(turned + 10 - zhi - turn) % 4 for turn in turns]
    ahead = [(turned + k + 6 - zhi) % 4 for k in returns]
    stage_at = [
        jnp.where(m == 0, 0, jnp.where(m == 2, 3, jnp.where(m == (4 + side) % 4, 1, 2))) for m in ahead
    ]
    place = jnp.stack(band_at + stage_at + [x, core, turned, zhi, side]).astype(jnp.int32)

    own = occupied.reshape(512, grid)
    partner, border = moved(with_partner), moved(with_border)
    band = send(targets.reshape(512, grid), moved(swapped))
    a1, b1 = send(own, partner), send(own, border)
    tables = call(
        table_kernel, [jax.ShapeDtypeStruct((2, 2 * grid, 2 * grid), jnp.bfloat16)] * 8,
        [smem, vmem], place, jnp.asarray(base_table()),
    )
    weights = screened_weights(chip * 16)
    a1, b1, weights, tables = lax.optimization_barrier((a1, b1, weights, tables))
    a2, b2 = send(b1, partner), send(a1, border)
    tables = dict(zip(names, tables))
    bands = [band] + [None] * 3
    for step in (2, 1, 3):
        bands[step] = send(band, along_y(step))
    a3, b3 = send(b2, partner), send(a2, border)
    a3, b3, bands[2] = lax.optimization_barrier((a3, b3, bands[2]))
    c4 = jnp.concatenate([send(b3[:256], partner), send(a3[256:], border)])
    owns, others = [own, b2, a2, c4], [a1, b1, a3, b3]

    blocks = call(
        functools.partial(density_kernel, 0, 3), [floats(384, grid)] * 8, [smem] + [vmem] * 12,
        place, *bands, own, a1, b2, b1, a2, a3, tables["z"], tables["y"],
    )
    blocks = call(
        functools.partial(density_kernel, 3, 1), [floats(512, grid)] * 8, [smem] + [vmem] * 16,
        place, *bands, c4, b3, tables["z"], tables["y"], *blocks,
    )
    arrived = exchange(blocks)
    back = call(
        convolve_kernel, [floats(512, grid)] * 8, [vmem] * 11,
        weights, tables["x"], tables["xi"], *arrived,
    )
    returned = exchange(back)
    sums = {}
    for first, count in parts:
        fields = call(
            functools.partial(field_kernel, first), [floats(512, grid)] * count, [smem] + [vmem] * 18,
            place, *returned, *owns, *others, tables["yi"], tables["zi"],
        )
        for k, field in zip(returns[first:], fields):
            sums[k] = send(field, along_y(k)) if k else field
    cells = send(after(sphere_map, sums[0]), moved(swapped)).reshape(1, 4096)
    picks = call(
        mask_kernel,
        [floats(512, grid), jax.ShapeDtypeStruct((grid, 4096), jnp.bfloat16), floats(32, 4096)],
        [vmem], cells,
    )
    sums[0], picks = lax.optimization_barrier((sums[0], picks))
    lines = call(
        applied_kernel, floats(32, 4, 8, grid), [vmem] * 6,
        *[sums[k] for k in range(4)], tables["z"], tables["y_end"],
    )
    lines = lax.all_to_all(lines, ("x", "y", "core"), 0, 0, tiled=True)
    picked = call(
        pick_kernel, floats(2, 4096), [vmem] * 5,
        lines.reshape(1024, grid), *picks, tables["x_end"],
    )
    return send(picked, moved(swapped_back))[None]


def solution(mesh):
    split = Mesh(mesh.devices.reshape(tuple(extent[a] for a in axes)), axes)
    bands, planes = ("zlo", "y"), ("x", "zhi", "core")
    return jax.shard_map(
        local,
        mesh=split,
        in_specs=(P(bands, planes, None, None), P(bands, planes, None, None), P(planes)),
        out_specs=P(bands, None, planes),
        check_vma=False,
    )
```

profile of v0, /device:TPU:65, one launch (start us, length us, event | category | flops | bytes accessed | tf_op | source)
XLA Modules:
  0.0 149.6 jit_solution(16148280442206739187)
XLA Ops:
  0.0 4.5 %collective-permute-start = (f32[512,128]{1,0:T(8,128)}, f32[512,128]{1,0:T(8,128)S(1)}, u32[]{:S(2)}, u32[]{:S(2)}) collective-permute-start(f32[512,128]{1,0:T(8,128)} %bitcast.28), channel_id=1, source_target_pairs={{0,128},{1,129},{2,130},{3,131},{4,132},{5,133},{6,134},{7,135},{8... | collective-permute-start | bytes 786440 | tf_op jit(solution)/shard_map/ppermute | solution.py:322
  4.5 2.9 %collective-permute-start.2 = (f32[512,128]{1,0:T(8,128)}, f32[512,128]{1,0:T(8,128)S(1)}, u32[]{:S(2)}, u32[]{:S(2)}) collective-permute-start(f32[512,128]{1,0:T(8,128)} %bitcast.36), channel_id=1, source_target_pairs={{0,64},{1,65},{2,96},{3,97},{4,0},{5,1},{6,32},{7,33},{8,72},{9,73... | collective-permute-start | bytes 786440 | tf_op jit(solution)/shard_map/ppermute | solution.py:322
  11.3 4.4 %collective-permute-start.4 = (f32[512,128]{1,0:T(8,128)S(1)}, f32[512,128]{1,0:T(8,128)S(1)}, u32[]{:S(2)}, u32[]{:S(2)}) collective-permute-start(f32[512,128]{1,0:T(8,128)S(1)} %collective-permute-done.refs_5_.refs_12_), channel_id=1, source_target_pairs={{0,134},{1,135},{2,128},{3,129},{4,130},{5,131},{6,132},{7,133},{8... | collective-permute-start | bytes 786440 | tf_op jit(solution)/shard_map/ppermute | solution.py:322
  17.0 3.2 %collective-permute-start.8 = (f32[512,128]{1,0:T(8,128)S(1)}, f32[512,128]{1,0:T(8,128)S(1)}, u32[]{:S(2)}, u32[]{:S(2)}) collective-permute-start(f32[512,128]{1,0:T(8,128)S(1)} %collective-permute-done.2.refs_0_), channel_id=1, source_target_pairs={{0,64},{1,65},{2,66},{3,67},{4,68},{5,69},{6,70},{7,71},{8,72},{9,... | collective-permute-start | bytes 786440 | tf_op jit(solution)/shard_map/ppermute | solution.py:322
  22.1 8.5 %collective-permute-start.7 = (f32[512,128]{1,0:T(8,128)S(1)}, f32[512,128]{1,0:T(8,128)S(1)}, u32[]{:S(2)}, u32[]{:S(2)}) collective-permute-start(f32[512,128]{1,0:T(8,128)S(1)} %collective-permute-done.6.refs_8_.refs_10_), channel_id=1, source_target_pairs={{0,134},{1,135},{2,128},{3,129},{4,130},{5,131},{6,132},{7,133},{8... | collective-permute-start | bytes 786440 | tf_op jit(solution)/shard_map/ppermute | solution.py:322
  32.7 2.8 %collective-permute-done.7.refs_5_.refs_15_ = f32[512,128]{1,0:T(8,128)S(1)} collective-permute-done((f32[512,128]{1,0:T(8,128)S(1)}, f32[512,128]{1,0:T(8,128)S(1)}, u32[]{:S(2)}, u32[]{:S(2)}) %collective-permute-start.7) | collective-permute-done | bytes 262176 | tf_op jit(solution)/shard_map/ppermute | solution.py:322
  35.7 2.7 %collective-permute-start.11 = (f32[256,128]{1,0:T(8,128)S(1)}, f32[256,128]{1,0:T(8,128)S(1)}, u32[]{:S(2)}, u32[]{:S(2)}) collective-permute-start(f32[256,128]{1,0:T(8,128)S(1)} %slice.7), channel_id=1, source_target_pairs={{0,134},{1,135},{2,128},{3,129},{4,130},{5,131},{6,132},{7,133},{8... | collective-permute-start | bytes 393224 | tf_op jit(solution)/shard_map/ppermute | solution.py:322
  39.9 2.4 %shard_map.47 = (f32[384,128]{1,0:T(8,128)S(1)}, f32[384,128]{1,0:T(8,128)S(1)}, f32[384,128]{1,0:T(8,128)S(1)}, f32[384,128]{1,0:T(8,128)S(1)}, f32[384,128]{1,...) custom-call(s32[13]{0:T(128)S(1)} %stack.55.place, ...), custom_call_target="tpu_custom_call" | custom-call | flops 1073741824 | bytes 1048576 | tf_op jit(solution)/shard_map/pallas_call | solution.py:256
  44.1 3.0 %collective-permute-start.12 = (f32[512,128]{1,0:T(8,128)S(1)}, f32[512,128]{1,0:T(8,128)S(1)}, u32[]{:S(2)}, u32[]{:S(2)}) collective-permute-start(f32[512,128]{1,0:T(8,128)S(1)} %get-tuple-element.88), channel_id=1, source_target_pairs={{0,16},{1,17},{2,18},{3,19},{4,20},{5,21},{6,22},{7,23},{8,24},{9,... | collective-permute-start | bytes 786440 | tf_op jit(solution)/shard_map/ppermute | solution.py:322
  47.1 3.1 %collective-permute-start.13 = (f32[512,128]{1,0:T(8,128)S(1)}, f32[512,128]{1,0:T(8,128)S(1)}, u32[]{:S(2)}, u32[]{:S(2)}) collective-permute-start(f32[512,128]{1,0:T(8,128)S(1)} %get-tuple-element.89), channel_id=1, source_target_pairs={{0,17},{1,16},{2,19},{3,18},{4,21},{5,20},{6,23},{7,22},{8,25},{9,... | collective-permute-start | bytes 786440 | tf_op jit(solution)/shard_map/ppermute | solution.py:322
  53.2 6.2 %collective-permute-start.17 = (f32[512,128]{1,0:T(8,128)S(1)}, f32[512,128]{1,0:T(8,128)S(1)}, u32[]{:S(2)}, u32[]{:S(2)}) collective-permute-start(f32[512,128]{1,0:T(8,128)S(1)} %get-tuple-element.93), channel_id=1, source_target_pairs={{0,25},{1,24},{2,27},{3,26},{4,29},{5,28},{6,31},{7,30},{8,1},{9,0... | collective-permute-start | bytes 786440 | tf_op jit(solution)/shard_map/ppermute | solution.py:322
  62.4 3.3 %collective-permute-done.14.refs_2_ = f32[512,128]{1,0:T(8,128)S(1)} collective-permute-done((f32[512,128]{1,0:T(8,128)S(1)}, f32[512,128]{1,0:T(8,128)S(1)}, u32[]{:S(2)}, u32[]{:S(2)}) %collective-permute-start.14) | collective-permute-done | bytes 262176 | tf_op jit(solution)/shard_map/ppermute | solution.py:322
  65.7 5.6 %collective-permute-done.15.refs_3_ = f32[512,128]{1,0:T(8,128)S(1)} collective-permute-done((f32[512,128]{1,0:T(8,128)S(1)}, f32[512,128]{1,0:T(8,128)S(1)}, u32[]{:S(2)}, u32[]{:S(2)}) %collective-permute-start.15) | collective-permute-done | bytes 262176 | tf_op jit(solution)/shard_map/ppermute | solution.py:322
  71.4 2.7 %shard_map.49 = (f32[512,128]{1,0:T(8,128)S(1)}, f32[512,128]{1,0:T(8,128)S(1)}, f32[512,128]{1,0:T(8,128)S(1)}, f32[512,128]{1,0:T(8,128)S(1)}, f32[512,128]{1,...) custom-call(f32[128,2048]{1,0:T(8,128)S(1)} %fusion.weights, ...), custom_call_target="tpu_custom_call" | custom-call | flops 1073741824 | bytes 1048576 | tf_op jit(solution)/shard_map/pallas_call | solution.py:256
  83.1 4.4 %collective-permute-start.24 = (f32[512,128]{1,0:T(8,128)S(1)}, f32[512,128]{1,0:T(8,128)S(1)}, u32[]{:S(2)}, u32[]{:S(2)}) collective-permute-start(f32[512,128]{1,0:T(8,128)S(1)} %get-tuple-element.101), channel_id=1, source_target_pairs={{0,25},{1,24},{2,27},{3,26},{4,29},{5,28},{6,31},{7,30},{8,1},{9,0... | collective-permute-start | bytes 786440 | tf_op jit(solution)/shard_map/ppermute | solution.py:322
  87.6 2.6 %collective-permute-done.20.refs_1_ = f32[512,128]{1,0:T(8,128)S(1)} collective-permute-done((f32[512,128]{1,0:T(8,128)S(1)}, f32[512,128]{1,0:T(8,128)S(1)}, u32[]{:S(2)}, u32[]{:S(2)}) %collective-permute-start.20) | collective-permute-done | bytes 262176 | tf_op jit(solution)/shard_map/ppermute | solution.py:322
  90.2 5.0 %collective-permute-done.21.refs_2_ = f32[512,128]{1,0:T(8,128)S(1)} collective-permute-done((f32[512,128]{1,0:T(8,128)S(1)}, f32[512,128]{1,0:T(8,128)S(1)}, u32[]{:S(2)}, u32[]{:S(2)}) %collective-permute-start.21) | collective-permute-done | bytes 262176 | tf_op jit(solution)/shard_map/ppermute | solution.py:322
  95.2 5.6 %collective-permute-done.22.refs_3_ = f32[512,128]{1,0:T(8,128)S(1)} collective-permute-done((f32[512,128]{1,0:T(8,128)S(1)}, f32[512,128]{1,0:T(8,128)S(1)}, u32[]{:S(2)}, u32[]{:S(2)}) %collective-permute-start.22) | collective-permute-done | bytes 262176 | tf_op jit(solution)/shard_map/ppermute | solution.py:322
  100.8 2.6 %shard_map.52 = (f32[512,128]{1,0:T(8,128)S(1)}, f32[512,128]{1,0:T(8,128)S(1)}, f32[512,128]{1,0:T(8,128)S(1)}) custom-call(s32[13]{0:T(128)S(1)} %stack.55.place, f32[512,128]{1,0:T(8,128)S(1)} %collective-permute-done.19.refs_0_, f32[512,128]{1,0:T(8,128)S(1)} %collective-permute-done.20.refs_1_, f32[512,128]{1,0:T(8,128)S(1)} %collective-permute-done.21.refs_2_, ...), custom_call_target="tpu_custom_call" | custom-call | flops 1073741824 | bytes 1048576 | tf_op jit(solution)/shard_map/pallas_call | solution.py:256
  103.8 3.8 %collective-permute-start.28 = (f32[512,128]{1,0:T(8,128)S(1)}, f32[512,128]{1,0:T(8,128)S(1)}, u32[]{:S(2)}, u32[]{:S(2)}) collective-permute-start(f32[512,128]{1,0:T(8,128)S(1)} %get-tuple-element.112), channel_id=1, source_target_pairs={{0,64},{1,65},{2,66},{3,67},{4,68},{5,69},{6,70},{7,71},{8,72},{9,... | collective-permute-start | bytes 786440 | tf_op jit(solution)/shard_map/ppermute | solution.py:322
  110.3 4.5 %collective-permute-done.26 = s32[4096]{0:T(1024)S(1)} collective-permute-done((s32[4096]{0:T(1024)S(1)}, s32[4096]{0:T(1024)S(1)}, u32[]{:S(2)}, u32[]{:S(2)}) %collective-permute-start.26) | collective-permute-done | bytes 16416 | tf_op jit(solution)/shard_map/ppermute | solution.py:322
  116.6 2.7 %collective-permute-done.28.two = f32[512,128]{1,0:T(8,128)S(1)} collective-permute-done((f32[512,128]{1,0:T(8,128)S(1)}, f32[512,128]{1,0:T(8,128)S(1)}, u32[]{:S(2)}, u32[]{:S(2)}) %collective-permute-start.28) | collective-permute-done | bytes 262176 | tf_op jit(solution)/shard_map/ppermute | solution.py:322
  120.3 20.9 %all_to_all.5 = f32[32,4,8,128]{3,2,1,0:T(8,128)S(1)} all-to-all(f32[32,4,8,128]{3,2,1,0:T(8,128)S(1)} %shard_map.53), channel_id=1, replica_groups=mesh['zlo'=2,'y'=4,'x'=4,'zhi'=4,'core'=2] {'x','y','core'}, dimensions={0} | all-to-all | bytes 1048576 | tf_op jit(solution)/shard_map/all_to_all | solution.py:417
  143.1 5.8 %collective-permute-done.30 = f32[2,4096]{1,0:T(2,128)S(1)} collective-permute-done((f32[2,4096]{1,0:T(2,128)S(1)}, f32[2,4096]{1,0:T(2,128)S(1)}, u32[]{:S(2)}, u32[]{:S(2)}) %collective-permute-start.30) | collective-permute-done | bytes 32800 | tf_op jit(solution)/shard_map/ppermute | solution.py:322
  (66 shorter events, 36.0 us)
Async XLA Ops:
  0.0 11.2 %collective-permute-start.1 = (f32[512,128]{1,0:T(8,128)}, f32[512,128]{1,0:T(8,128)S(1)}, u32[]{:S(2)}, u32[]{:S(2)}) collective-permute-start(f32[512,128]{1,0:T(8,128)} %bitcast.27), channel_id=1, source_target_pairs={{0,134},{1,135},{2,128},{3,129},{4,130},{5,131},{6,132},{7,133},{8... | collective-permute-start | bytes 786440 | tf_op jit(solution)/shard_map/ppermute | solution.py:322
  0.0 11.2 %collective-permute-start = (f32[512,128]{1,0:T(8,128)}, f32[512,128]{1,0:T(8,128)S(1)}, u32[]{:S(2)}, u32[]{:S(2)}) collective-permute-start(f32[512,128]{1,0:T(8,128)} %bitcast.28), channel_id=1, source_target_pairs={{0,128},{1,129},{2,130},{3,131},{4,132},{5,133},{6,134},{7,135},{8... | collective-permute-start | bytes 786440 | tf_op jit(solution)/shard_map/ppermute | solution.py:322
  4.5 12.5 %collective-permute-start.2 = (f32[512,128]{1,0:T(8,128)}, f32[512,128]{1,0:T(8,128)S(1)}, u32[]{:S(2)}, u32[]{:S(2)}) collective-permute-start(f32[512,128]{1,0:T(8,128)} %bitcast.36), channel_id=1, source_target_pairs={{0,64},{1,65},{2,96},{3,97},{4,0},{5,1},{6,32},{7,33},{8,72},{9,73... | collective-permute-start | bytes 786440 | tf_op jit(solution)/shard_map/ppermute | solution.py:322
  11.3 8.9 %collective-permute-start.4 = (f32[512,128]{1,0:T(8,128)S(1)}, f32[512,128]{1,0:T(8,128)S(1)}, u32[]{:S(2)}, u32[]{:S(2)}) collective-permute-start(f32[512,128]{1,0:T(8,128)S(1)} %collective-permute-done.refs_5_.refs_12_), channel_id=1, source_target_pairs={{0,134},{1,135},{2,128},{3,129},{4,130},{5,131},{6,132},{7,133},{8... | collective-permute-start | bytes 786440 | tf_op jit(solution)/shard_map/ppermute | solution.py:322
  17.0 15.7 %collective-permute-start.8 = (f32[512,128]{1,0:T(8,128)S(1)}, f32[512,128]{1,0:T(8,128)S(1)}, u32[]{:S(2)}, u32[]{:S(2)}) collective-permute-start(f32[512,128]{1,0:T(8,128)S(1)} %collective-permute-done.2.refs_0_), channel_id=1, source_target_pairs={{0,64},{1,65},{2,66},{3,67},{4,68},{5,69},{6,70},{7,71},{8,72},{9,... | collective-permute-start | bytes 786440 | tf_op jit(solution)/shard_map/ppermute | solution.py:322
  20.2 12.5 %collective-permute-start.5 = (f32[512,128]{1,0:T(8,128)S(1)}, f32[512,128]{1,0:T(8,128)S(1)}, u32[]{:S(2)}, u32[]{:S(2)}) collective-permute-start(f32[512,128]{1,0:T(8,128)S(1)} %collective-permute-done.4.refs_6_.refs_9_), channel_id=1, source_target_pairs={{0,128},{1,129},{2,130},{3,131},{4,132},{5,133},{6,134},{7,135},{8... | collective-permute-start | bytes 786440 | tf_op jit(solution)/shard_map/ppermute | solution.py:322
  22.1 13.5 %collective-permute-start.7 = (f32[512,128]{1,0:T(8,128)S(1)}, f32[512,128]{1,0:T(8,128)S(1)}, u32[]{:S(2)}, u32[]{:S(2)}) collective-permute-start(f32[512,128]{1,0:T(8,128)S(1)} %collective-permute-done.6.refs_8_.refs_10_), channel_id=1, source_target_pairs={{0,134},{1,135},{2,128},{3,129},{4,130},{5,131},{6,132},{7,133},{8... | collective-permute-start | bytes 786440 | tf_op jit(solution)/shard_map/ppermute | solution.py:322
  44.1 9.2 %collective-permute-start.12 = (f32[512,128]{1,0:T(8,128)S(1)}, f32[512,128]{1,0:T(8,128)S(1)}, u32[]{:S(2)}, u32[]{:S(2)}) collective-permute-start(f32[512,128]{1,0:T(8,128)S(1)} %get-tuple-element.88), channel_id=1, source_target_pairs={{0,16},{1,17},{2,18},{3,19},{4,20},{5,21},{6,22},{7,23},{8,24},{9,... | collective-permute-start | bytes 786440 | tf_op jit(solution)/shard_map/ppermute | solution.py:322
  47.1 13.1 %collective-permute-start.13 = (f32[512,128]{1,0:T(8,128)S(1)}, f32[512,128]{1,0:T(8,128)S(1)}, u32[]{:S(2)}, u32[]{:S(2)}) collective-permute-start(f32[512,128]{1,0:T(8,128)S(1)} %get-tuple-element.89), channel_id=1, source_target_pairs={{0,17},{1,16},{2,19},{3,18},{4,21},{5,20},{6,23},{7,22},{8,25},{9,... | collective-permute-start | bytes 786440 | tf_op jit(solution)/shard_map/ppermute | solution.py:322
  50.2 15.5 %collective-permute-start.14 = (f32[512,128]{1,0:T(8,128)S(1)}, f32[512,128]{1,0:T(8,128)S(1)}, u32[]{:S(2)}, u32[]{:S(2)}) collective-permute-start(f32[512,128]{1,0:T(8,128)S(1)} %get-tuple-element.90), channel_id=1, source_target_pairs={{0,8},{1,9},{2,10},{3,11},{4,12},{5,13},{6,14},{7,15},{8,16},{9,17... | collective-permute-start | bytes 786440 | tf_op jit(solution)/shard_map/ppermute | solution.py:322
  51.4 20.0 %collective-permute-start.15 = (f32[512,128]{1,0:T(8,128)S(1)}, f32[512,128]{1,0:T(8,128)S(1)}, u32[]{:S(2)}, u32[]{:S(2)}) collective-permute-start(f32[512,128]{1,0:T(8,128)S(1)} %get-tuple-element.91), channel_id=1, source_target_pairs={{0,9},{1,8},{2,11},{3,10},{4,13},{5,12},{6,15},{7,14},{8,17},{9,16... | collective-permute-start | bytes 786440 | tf_op jit(solution)/shard_map/ppermute | solution.py:322
  51.4 20.0 %collective-permute-start.16 = (f32[512,128]{1,0:T(8,128)S(1)}, f32[512,128]{1,0:T(8,128)S(1)}, u32[]{:S(2)}, u32[]{:S(2)}) collective-permute-start(f32[512,128]{1,0:T(8,128)S(1)} %get-tuple-element.92), channel_id=1, source_target_pairs={{0,24},{1,25},{2,26},{3,27},{4,28},{5,29},{6,30},{7,31},{8,0},{9,1... | collective-permute-start | bytes 786440 | tf_op jit(solution)/shard_map/ppermute | solution.py:322
  53.2 18.1 %collective-permute-start.17 = (f32[512,128]{1,0:T(8,128)S(1)}, f32[512,128]{1,0:T(8,128)S(1)}, u32[]{:S(2)}, u32[]{:S(2)}) collective-permute-start(f32[512,128]{1,0:T(8,128)S(1)} %get-tuple-element.93), channel_id=1, source_target_pairs={{0,25},{1,24},{2,27},{3,26},{4,29},{5,28},{6,31},{7,30},{8,1},{9,0... | collective-permute-start | bytes 786440 | tf_op jit(solution)/shard_map/ppermute | solution.py:322
  60.2 11.2 %collective-permute-start.18 = (f32[512,128]{1,0:T(8,128)S(1)}, f32[512,128]{1,0:T(8,128)S(1)}, u32[]{:S(2)}, u32[]{:S(2)}) collective-permute-start(f32[512,128]{1,0:T(8,128)S(1)} %get-tuple-element.95), channel_id=1, source_target_pairs={{0,1},{1,0},{2,3},{3,2},{4,5},{5,4},{6,7},{7,6},{8,9},{9,8},{10,11... | collective-permute-start | bytes 786440 | tf_op jit(solution)/shard_map/ppermute | solution.py:322
  74.0 9.1 %collective-permute-start.19 = (f32[512,128]{1,0:T(8,128)S(1)}, f32[512,128]{1,0:T(8,128)S(1)}, u32[]{:S(2)}, u32[]{:S(2)}) collective-permute-start(f32[512,128]{1,0:T(8,128)S(1)} %get-tuple-element.96), channel_id=1, source_target_pairs={{0,16},{1,17},{2,18},{3,19},{4,20},{5,21},{6,22},{7,23},{8,24},{9,... | collective-permute-start | bytes 786440 | tf_op jit(solution)/shard_map/ppermute | solution.py:322
  76.2 13.9 %collective-permute-start.20 = (f32[512,128]{1,0:T(8,128)S(1)}, f32[512,128]{1,0:T(8,128)S(1)}, u32[]{:S(2)}, u32[]{:S(2)}) collective-permute-start(f32[512,128]{1,0:T(8,128)S(1)} %get-tuple-element.97), channel_id=1, source_target_pairs={{0,17},{1,16},{2,19},{3,18},{4,21},{5,20},{6,23},{7,22},{8,25},{9,... | collective-permute-start | bytes 786440 | tf_op jit(solution)/shard_map/ppermute | solution.py:322
  77.7 17.5 %collective-permute-start.21 = (f32[512,128]{1,0:T(8,128)S(1)}, f32[512,128]{1,0:T(8,128)S(1)}, u32[]{:S(2)}, u32[]{:S(2)}) collective-permute-start(f32[512,128]{1,0:T(8,128)S(1)} %get-tuple-element.98), channel_id=1, source_target_pairs={{0,8},{1,9},{2,10},{3,11},{4,12},{5,13},{6,14},{7,15},{8,16},{9,17... | collective-permute-start | bytes 786440 | tf_op jit(solution)/shard_map/ppermute | solution.py:322
  78.8 22.0 %collective-permute-start.22 = (f32[512,128]{1,0:T(8,128)S(1)}, f32[512,128]{1,0:T(8,128)S(1)}, u32[]{:S(2)}, u32[]{:S(2)}) collective-permute-start(f32[512,128]{1,0:T(8,128)S(1)} %get-tuple-element.99), channel_id=1, source_target_pairs={{0,9},{1,8},{2,11},{3,10},{4,13},{5,12},{6,15},{7,14},{8,17},{9,16... | collective-permute-start | bytes 786440 | tf_op jit(solution)/shard_map/ppermute | solution.py:322
  79.4 21.4 %collective-permute-start.23 = (f32[512,128]{1,0:T(8,128)S(1)}, f32[512,128]{1,0:T(8,128)S(1)}, u32[]{:S(2)}, u32[]{:S(2)}) collective-permute-start(f32[512,128]{1,0:T(8,128)S(1)} %get-tuple-element.100), channel_id=1, source_target_pairs={{0,24},{1,25},{2,26},{3,27},{4,28},{5,29},{6,30},{7,31},{8,0},{9,1... | collective-permute-start | bytes 786440 | tf_op jit(solution)/shard_map/ppermute | solution.py:322
  83.1 17.7 %collective-permute-start.24 = (f32[512,128]{1,0:T(8,128)S(1)}, f32[512,128]{1,0:T(8,128)S(1)}, u32[]{:S(2)}, u32[]{:S(2)}) collective-permute-start(f32[512,128]{1,0:T(8,128)S(1)} %get-tuple-element.101), channel_id=1, source_target_pairs={{0,25},{1,24},{2,27},{3,26},{4,29},{5,28},{6,31},{7,30},{8,1},{9,0... | collective-permute-start | bytes 786440 | tf_op jit(solution)/shard_map/ppermute | solution.py:322
  90.1 10.6 %collective-permute-start.25 = (f32[512,128]{1,0:T(8,128)S(1)}, f32[512,128]{1,0:T(8,128)S(1)}, u32[]{:S(2)}, u32[]{:S(2)}) collective-permute-start(f32[512,128]{1,0:T(8,128)S(1)} %get-tuple-element.103), channel_id=1, source_target_pairs={{0,1},{1,0},{2,3},{3,2},{4,5},{5,4},{6,7},{7,6},{8,9},{9,8},{10,11... | collective-permute-start | bytes 786440 | tf_op jit(solution)/shard_map/ppermute | solution.py:322
  103.4 13.2 %collective-permute-start.27 = (f32[512,128]{1,0:T(8,128)S(1)}, f32[512,128]{1,0:T(8,128)S(1)}, u32[]{:S(2)}, u32[]{:S(2)}) collective-permute-start(f32[512,128]{1,0:T(8,128)S(1)} %get-tuple-element.111), channel_id=1, source_target_pairs={{0,32},{1,33},{2,34},{3,35},{4,36},{5,37},{6,38},{7,39},{8,40},{9,... | collective-permute-start | bytes 786440 | tf_op jit(solution)/shard_map/ppermute | solution.py:322
  103.8 15.4 %collective-permute-start.28 = (f32[512,128]{1,0:T(8,128)S(1)}, f32[512,128]{1,0:T(8,128)S(1)}, u32[]{:S(2)}, u32[]{:S(2)}) collective-permute-start(f32[512,128]{1,0:T(8,128)S(1)} %get-tuple-element.112), channel_id=1, source_target_pairs={{0,64},{1,65},{2,66},{3,67},{4,68},{5,69},{6,70},{7,71},{8,72},{9,... | collective-permute-start | bytes 786440 | tf_op jit(solution)/shard_map/ppermute | solution.py:322
  107.6 11.6 %collective-permute-start.29 = (f32[512,128]{1,0:T(8,128)S(1)}, f32[512,128]{1,0:T(8,128)S(1)}, u32[]{:S(2)}, u32[]{:S(2)}) collective-permute-start(f32[512,128]{1,0:T(8,128)S(1)} %get-tuple-element.113), channel_id=1, source_target_pairs={{0,96},{1,97},{2,98},{3,99},{4,100},{5,101},{6,102},{7,103},{8,104... | collective-permute-start | bytes 786440 | tf_op jit(solution)/shard_map/ppermute | solution.py:322
  (10 other events, 78.0 us)
where the time goes:
time: 150 us
  starting transfers between devices  65.7 us (44%)
  waiting for transfers between devices  43.3 us (29%)
  blocking collectives  20.9 us (14%)
  Pallas kernels  16.8 us (11%)
  local copies, waits for them, and re-layouts  1.81 us (1%)
    ppermute x31, starting transfers between devices, send(): return lax.ppermute(value, axes, pairs)  65.7 us
    ppermute x31, waiting for transfers between devices, send(): return lax.ppermute(value, axes, pairs)  43.3 us
    all_to_all x1, blocking collectives, local(): lines = lax.all_to_all(lines, ('x', 'y', 'core'), 0, 0, tiled=True)  20.9 us
    pallas_call x9, Pallas kernels, call(): pl.pallas_call(kernel, out_shape=shapes, in_specs=specs, out_specs=jax.tr...  16.8 us
  transfers between devices with their start and end apart: 31, of which 13 were waited for; matrix products, arithmetic and copies ran while one was open for 1% of the time, Pallas kernels for 5%

commit v1 on v0

--- a/solution.py
+++ b/solution.py
@@ -37,7 +37,7 @@
 
 
 names = ("z", "zi", "y", "yi", "x", "xi", "y_end", "x_end")
-steps = tuple((r, c) for r in (2, 1, 3, 0) for c in (0, 1))
+steps = ((2, 0), (2, 1), (1, 0), (3, 0), (1, 1), (3, 1), (0, 0), (0, 1))
 returns = (2, 1, 3, 0)
 parts = ((0, 3), (3, 1))
 
@@ -99,8 +99,8 @@
         return (goal == index).astype(jnp.bfloat16)
 
     step = at >> 5
-    far = pick(step >> 1, (2, 1, 3, 0))
-    twin = (core + step) & 1
+    far = pick(step, [r for r, _ in steps])
+    twin = (core + pick(step, [c for _, c in steps])) & 1
 
     def block(sign):
         chip = ((x + 4 + sign * far) & 3) * 2 + twin

time: 150 us -> 150 us (level)
  no operation moved by 1% of the time
where the time goes in v1:
time: 150 us
  starting transfers between devices  64.7 us (43%)
  waiting for transfers between devices  44.2 us (29%)
  blocking collectives  21 us (14%)
  Pallas kernels  16.8 us (11%)
  local copies, waits for them, and re-layouts  1.81 us (1%)
    ppermute x31, starting transfers between devices, send(): return lax.ppermute(value, axes, pairs)  64.7 us
    ppermute x31, waiting for transfers between devices, send(): return lax.ppermute(value, axes, pairs)  44.2 us
    all_to_all x1, blocking collectives, local(): lines = lax.all_to_all(lines, ('x', 'y', 'core'), 0, 0, tiled=True)  21 us
    pallas_call x9, Pallas kernels, call(): pl.pallas_call(kernel, out_shape=shapes, in_specs=specs, out_specs=jax.tr...  16.8 us
  transfers between devices with their start and end apart: 31, of which 13 were waited for; matrix products, arithmetic and copies ran while one was open for 1% of the time, Pallas kernels for 5%

profile of v1, /device:TPU:65, one launch (start us, length us, event | category | flops | bytes accessed | tf_op | source)
XLA Modules:
  0.0 149.6 jit_solution(5118625585059036662)
XLA Ops:
  0.0 4.5 %collective-permute-start = (f32[512,128]{1,0:T(8,128)}, f32[512,128]{1,0:T(8,128)S(1)}, u32[]{:S(2)}, u32[]{:S(2)}) collective-permute-start(f32[512,128]{1,0:T(8,128)} %bitcast.28), channel_id=1, source_target_pairs={{0,128},{1,129},{2,130},{3,131},{4,132},{5,133},{6,134},{7,135},{8... | collective-permute-start | bytes 786440 | tf_op jit(solution)/shard_map/ppermute | solution.py:322
  4.5 2.9 %collective-permute-start.2 = (f32[512,128]{1,0:T(8,128)}, f32[512,128]{1,0:T(8,128)S(1)}, u32[]{:S(2)}, u32[]{:S(2)}) collective-permute-start(f32[512,128]{1,0:T(8,128)} %bitcast.36), channel_id=1, source_target_pairs={{0,64},{1,65},{2,96},{3,97},{4,0},{5,1},{6,32},{7,33},{8,72},{9,73... | collective-permute-start | bytes 786440 | tf_op jit(solution)/shard_map/ppermute | solution.py:322
  11.3 4.4 %collective-permute-start.4 = (f32[512,128]{1,0:T(8,128)S(1)}, f32[512,128]{1,0:T(8,128)S(1)}, u32[]{:S(2)}, u32[]{:S(2)}) collective-permute-start(f32[512,128]{1,0:T(8,128)S(1)} %collective-permute-done.refs_5_.refs_12_), channel_id=1, source_target_pairs={{0,134},{1,135},{2,128},{3,129},{4,130},{5,131},{6,132},{7,133},{8... | collective-permute-start | bytes 786440 | tf_op jit(solution)/shard_map/ppermute | solution.py:322
  17.0 3.2 %collective-permute-start.8 = (f32[512,128]{1,0:T(8,128)S(1)}, f32[512,128]{1,0:T(8,128)S(1)}, u32[]{:S(2)}, u32[]{:S(2)}) collective-permute-start(f32[512,128]{1,0:T(8,128)S(1)} %collective-permute-done.2.refs_0_), channel_id=1, source_target_pairs={{0,64},{1,65},{2,66},{3,67},{4,68},{5,69},{6,70},{7,71},{8,72},{9,... | collective-permute-start | bytes 786440 | tf_op jit(solution)/shard_map/ppermute | solution.py:322
  22.1 8.5 %collective-permute-start.7 = (f32[512,128]{1,0:T(8,128)S(1)}, f32[512,128]{1,0:T(8,128)S(1)}, u32[]{:S(2)}, u32[]{:S(2)}) collective-permute-start(f32[512,128]{1,0:T(8,128)S(1)} %collective-permute-done.6.refs_8_.refs_10_), channel_id=1, source_target_pairs={{0,134},{1,135},{2,128},{3,129},{4,130},{5,131},{6,132},{7,133},{8... | collective-permute-start | bytes 786440 | tf_op jit(solution)/shard_map/ppermute | solution.py:322
  32.7 2.8 %collective-permute-done.7.refs_5_.refs_15_ = f32[512,128]{1,0:T(8,128)S(1)} collective-permute-done((f32[512,128]{1,0:T(8,128)S(1)}, f32[512,128]{1,0:T(8,128)S(1)}, u32[]{:S(2)}, u32[]{:S(2)}) %collective-permute-start.7) | collective-permute-done | bytes 262176 | tf_op jit(solution)/shard_map/ppermute | solution.py:322
  35.7 2.7 %collective-permute-start.11 = (f32[256,128]{1,0:T(8,128)S(1)}, f32[256,128]{1,0:T(8,128)S(1)}, u32[]{:S(2)}, u32[]{:S(2)}) collective-permute-start(f32[256,128]{1,0:T(8,128)S(1)} %slice.7), channel_id=1, source_target_pairs={{0,134},{1,135},{2,128},{3,129},{4,130},{5,131},{6,132},{7,133},{8... | collective-permute-start | bytes 393224 | tf_op jit(solution)/shard_map/ppermute | solution.py:322
  44.1 3.0 %collective-permute-start.12 = (f32[512,128]{1,0:T(8,128)S(1)}, f32[512,128]{1,0:T(8,128)S(1)}, u32[]{:S(2)}, u32[]{:S(2)}) collective-permute-start(f32[512,128]{1,0:T(8,128)S(1)} %get-tuple-element.88), channel_id=1, source_target_pairs={{0,16},{1,17},{2,18},{3,19},{4,20},{5,21},{6,22},{7,23},{8,24},{9,... | collective-permute-start | bytes 786440 | tf_op jit(solution)/shard_map/ppermute | solution.py:322
  47.1 3.1 %collective-permute-start.13 = (f32[512,128]{1,0:T(8,128)S(1)}, f32[512,128]{1,0:T(8,128)S(1)}, u32[]{:S(2)}, u32[]{:S(2)}) collective-permute-start(f32[512,128]{1,0:T(8,128)S(1)} %get-tuple-element.89), channel_id=1, source_target_pairs={{0,17},{1,16},{2,19},{3,18},{4,21},{5,20},{6,23},{7,22},{8,25},{9,... | collective-permute-start | bytes 786440 | tf_op jit(solution)/shard_map/ppermute | solution.py:322
  52.9 6.5 %collective-permute-start.17 = (f32[512,128]{1,0:T(8,128)S(1)}, f32[512,128]{1,0:T(8,128)S(1)}, u32[]{:S(2)}, u32[]{:S(2)}) collective-permute-start(f32[512,128]{1,0:T(8,128)S(1)} %get-tuple-element.93), channel_id=1, source_target_pairs={{0,25},{1,24},{2,27},{3,26},{4,29},{5,28},{6,31},{7,30},{8,1},{9,0... | collective-permute-start | bytes 786440 | tf_op jit(solution)/shard_map/ppermute | solution.py:322
  62.4 3.3 %collective-permute-done.14.refs_2_ = f32[512,128]{1,0:T(8,128)S(1)} collective-permute-done((f32[512,128]{1,0:T(8,128)S(1)}, f32[512,128]{1,0:T(8,128)S(1)}, u32[]{:S(2)}, u32[]{:S(2)}) %collective-permute-start.14) | collective-permute-done | bytes 262176 | tf_op jit(solution)/shard_map/ppermute | solution.py:322
  65.7 5.6 %collective-permute-done.16.refs_4_ = f32[512,128]{1,0:T(8,128)S(1)} collective-permute-done((f32[512,128]{1,0:T(8,128)S(1)}, f32[512,128]{1,0:T(8,128)S(1)}, u32[]{:S(2)}, u32[]{:S(2)}) %collective-permute-start.16) | collective-permute-done | bytes 262176 | tf_op jit(solution)/shard_map/ppermute | solution.py:322
  71.4 2.7 %shard_map.49 = (f32[512,128]{1,0:T(8,128)S(1)}, f32[512,128]{1,0:T(8,128)S(1)}, f32[512,128]{1,0:T(8,128)S(1)}, f32[512,128]{1,0:T(8,128)S(1)}, f32[512,128]{1,...) custom-call(f32[128,2048]{1,0:T(8,128)S(1)} %fusion.weights, ...), custom_call_target="tpu_custom_call" | custom-call | flops 1073741824 | bytes 1048576 | tf_op jit(solution)/shard_map/pallas_call | solution.py:256
  80.6 2.5 %collective-permute-done.19.refs_0_ = f32[512,128]{1,0:T(8,128)S(1)} collective-permute-done((f32[512,128]{1,0:T(8,128)S(1)}, f32[512,128]{1,0:T(8,128)S(1)}, u32[]{:S(2)}, u32[]{:S(2)}) %collective-permute-start.19) | collective-permute-done | bytes 262176 | tf_op jit(solution)/shard_map/ppermute | solution.py:322
  83.1 4.5 %collective-permute-start.24 = (f32[512,128]{1,0:T(8,128)S(1)}, f32[512,128]{1,0:T(8,128)S(1)}, u32[]{:S(2)}, u32[]{:S(2)}) collective-permute-start(f32[512,128]{1,0:T(8,128)S(1)} %get-tuple-element.101), channel_id=1, source_target_pairs={{0,25},{1,24},{2,27},{3,26},{4,29},{5,28},{6,31},{7,30},{8,1},{9,0... | collective-permute-start | bytes 786440 | tf_op jit(solution)/shard_map/ppermute | solution.py:322
  87.6 2.5 %collective-permute-done.20.refs_1_ = f32[512,128]{1,0:T(8,128)S(1)} collective-permute-done((f32[512,128]{1,0:T(8,128)S(1)}, f32[512,128]{1,0:T(8,128)S(1)}, u32[]{:S(2)}, u32[]{:S(2)}) %collective-permute-start.20) | collective-permute-done | bytes 262176 | tf_op jit(solution)/shard_map/ppermute | solution.py:322
  90.1 5.0 %collective-permute-done.21.refs_2_ = f32[512,128]{1,0:T(8,128)S(1)} collective-permute-done((f32[512,128]{1,0:T(8,128)S(1)}, f32[512,128]{1,0:T(8,128)S(1)}, u32[]{:S(2)}, u32[]{:S(2)}) %collective-permute-start.21) | collective-permute-done | bytes 262176 | tf_op jit(solution)/shard_map/ppermute | solution.py:322
  95.2 5.6 %collective-permute-done.23.refs_4_ = f32[512,128]{1,0:T(8,128)S(1)} collective-permute-done((f32[512,128]{1,0:T(8,128)S(1)}, f32[512,128]{1,0:T(8,128)S(1)}, u32[]{:S(2)}, u32[]{:S(2)}) %collective-permute-start.23) | collective-permute-done | bytes 262176 | tf_op jit(solution)/shard_map/ppermute | solution.py:322
  100.8 2.6 %shard_map.52 = (f32[512,128]{1,0:T(8,128)S(1)}, f32[512,128]{1,0:T(8,128)S(1)}, f32[512,128]{1,0:T(8,128)S(1)}) custom-call(s32[13]{0:T(128)S(1)} %stack.55.place, f32[512,128]{1,0:T(8,128)S(1)} %collective-permute-done.19.refs_0_, f32[512,128]{1,0:T(8,128)S(1)} %collective-permute-done.20.refs_1_, f32[512,128]{1,0:T(8,128)S(1)} %collective-permute-done.21.refs_2_, ...), custom_call_target="tpu_custom_call" | custom-call | flops 1073741824 | bytes 1048576 | tf_op jit(solution)/shard_map/pallas_call | solution.py:256
  103.8 3.8 %collective-permute-start.28 = (f32[512,128]{1,0:T(8,128)S(1)}, f32[512,128]{1,0:T(8,128)S(1)}, u32[]{:S(2)}, u32[]{:S(2)}) collective-permute-start(f32[512,128]{1,0:T(8,128)S(1)} %get-tuple-element.112), channel_id=1, source_target_pairs={{0,64},{1,65},{2,66},{3,67},{4,68},{5,69},{6,70},{7,71},{8,72},{9,... | collective-permute-start | bytes 786440 | tf_op jit(solution)/shard_map/ppermute | solution.py:322
  110.2 4.5 %collective-permute-done.26 = s32[4096]{0:T(1024)S(1)} collective-permute-done((s32[4096]{0:T(1024)S(1)}, s32[4096]{0:T(1024)S(1)}, u32[]{:S(2)}, u32[]{:S(2)}) %collective-permute-start.26) | collective-permute-done | bytes 16416 | tf_op jit(solution)/shard_map/ppermute | solution.py:322
  116.6 2.7 %collective-permute-done.28.two = f32[512,128]{1,0:T(8,128)S(1)} collective-permute-done((f32[512,128]{1,0:T(8,128)S(1)}, f32[512,128]{1,0:T(8,128)S(1)}, u32[]{:S(2)}, u32[]{:S(2)}) %collective-permute-start.28) | collective-permute-done | bytes 262176 | tf_op jit(solution)/shard_map/ppermute | solution.py:322
  120.3 21.0 %all_to_all.5 = f32[32,4,8,128]{3,2,1,0:T(8,128)S(1)} all-to-all(f32[32,4,8,128]{3,2,1,0:T(8,128)S(1)} %shard_map.53), channel_id=1, replica_groups=mesh['zlo'=2,'y'=4,'x'=4,'zhi'=4,'core'=2] {'x','y','core'}, dimensions={0} | all-to-all | bytes 1048576 | tf_op jit(solution)/shard_map/all_to_all | solution.py:417
  143.2 5.8 %collective-permute-done.30 = f32[2,4096]{1,0:T(2,128)S(1)} collective-permute-done((f32[2,4096]{1,0:T(2,128)S(1)}, f32[2,4096]{1,0:T(2,128)S(1)}, u32[]{:S(2)}, u32[]{:S(2)}) %collective-permute-start.30) | collective-permute-done | bytes 32800 | tf_op jit(solution)/shard_map/ppermute | solution.py:322
  (66 shorter events, 35.6 us)
Async XLA Ops:
  0.0 11.3 %collective-permute-start.1 = (f32[512,128]{1,0:T(8,128)}, f32[512,128]{1,0:T(8,128)S(1)}, u32[]{:S(2)}, u32[]{:S(2)}) collective-permute-start(f32[512,128]{1,0:T(8,128)} %bitcast.27), channel_id=1, source_target_pairs={{0,134},{1,135},{2,128},{3,129},{4,130},{5,131},{6,132},{7,133},{8... | collective-permute-start | bytes 786440 | tf_op jit(solution)/shard_map/ppermute | solution.py:322
  0.0 11.3 %collective-permute-start = (f32[512,128]{1,0:T(8,128)}, f32[512,128]{1,0:T(8,128)S(1)}, u32[]{:S(2)}, u32[]{:S(2)}) collective-permute-start(f32[512,128]{1,0:T(8,128)} %bitcast.28), channel_id=1, source_target_pairs={{0,128},{1,129},{2,130},{3,131},{4,132},{5,133},{6,134},{7,135},{8... | collective-permute-start | bytes 786440 | tf_op jit(solution)/shard_map/ppermute | solution.py:322
  4.5 12.5 %collective-permute-start.2 = (f32[512,128]{1,0:T(8,128)}, f32[512,128]{1,0:T(8,128)S(1)}, u32[]{:S(2)}, u32[]{:S(2)}) collective-permute-start(f32[512,128]{1,0:T(8,128)} %bitcast.36), channel_id=1, source_target_pairs={{0,64},{1,65},{2,96},{3,97},{4,0},{5,1},{6,32},{7,33},{8,72},{9,73... | collective-permute-start | bytes 786440 | tf_op jit(solution)/shard_map/ppermute | solution.py:322
  11.3 8.8 %collective-permute-start.4 = (f32[512,128]{1,0:T(8,128)S(1)}, f32[512,128]{1,0:T(8,128)S(1)}, u32[]{:S(2)}, u32[]{:S(2)}) collective-permute-start(f32[512,128]{1,0:T(8,128)S(1)} %collective-permute-done.refs_5_.refs_12_), channel_id=1, source_target_pairs={{0,134},{1,135},{2,128},{3,129},{4,130},{5,131},{6,132},{7,133},{8... | collective-permute-start | bytes 786440 | tf_op jit(solution)/shard_map/ppermute | solution.py:322
  17.0 15.7 %collective-permute-start.8 = (f32[512,128]{1,0:T(8,128)S(1)}, f32[512,128]{1,0:T(8,128)S(1)}, u32[]{:S(2)}, u32[]{:S(2)}) collective-permute-start(f32[512,128]{1,0:T(8,128)S(1)} %collective-permute-done.2.refs_0_), channel_id=1, source_target_pairs={{0,64},{1,65},{2,66},{3,67},{4,68},{5,69},{6,70},{7,71},{8,72},{9,... | collective-permute-start | bytes 786440 | tf_op jit(solution)/shard_map/ppermute | solution.py:322
  20.2 12.5 %collective-permute-start.5 = (f32[512,128]{1,0:T(8,128)S(1)}, f32[512,128]{1,0:T(8,128)S(1)}, u32[]{:S(2)}, u32[]{:S(2)}) collective-permute-start(f32[512,128]{1,0:T(8,128)S(1)} %collective-permute-done.4.refs_6_.refs_9_), channel_id=1, source_target_pairs={{0,128},{1,129},{2,130},{3,131},{4,132},{5,133},{6,134},{7,135},{8... | collective-permute-start | bytes 786440 | tf_op jit(solution)/shard_map/ppermute | solution.py:322
  22.1 13.5 %collective-permute-start.7 = (f32[512,128]{1,0:T(8,128)S(1)}, f32[512,128]{1,0:T(8,128)S(1)}, u32[]{:S(2)}, u32[]{:S(2)}) collective-permute-start(f32[512,128]{1,0:T(8,128)S(1)} %collective-permute-done.6.refs_8_.refs_10_), channel_id=1, source_target_pairs={{0,134},{1,135},{2,128},{3,129},{4,130},{5,131},{6,132},{7,133},{8... | collective-permute-start | bytes 786440 | tf_op jit(solution)/shard_map/ppermute | solution.py:322
  44.1 8.8 %collective-permute-start.12 = (f32[512,128]{1,0:T(8,128)S(1)}, f32[512,128]{1,0:T(8,128)S(1)}, u32[]{:S(2)}, u32[]{:S(2)}) collective-permute-start(f32[512,128]{1,0:T(8,128)S(1)} %get-tuple-element.88), channel_id=1, source_target_pairs={{0,16},{1,17},{2,18},{3,19},{4,20},{5,21},{6,22},{7,23},{8,24},{9,... | collective-permute-start | bytes 786440 | tf_op jit(solution)/shard_map/ppermute | solution.py:322
  47.1 13.1 %collective-permute-start.13 = (f32[512,128]{1,0:T(8,128)S(1)}, f32[512,128]{1,0:T(8,128)S(1)}, u32[]{:S(2)}, u32[]{:S(2)}) collective-permute-start(f32[512,128]{1,0:T(8,128)S(1)} %get-tuple-element.89), channel_id=1, source_target_pairs={{0,17},{1,16},{2,19},{3,18},{4,21},{5,20},{6,23},{7,22},{8,25},{9,... | collective-permute-start | bytes 786440 | tf_op jit(solution)/shard_map/ppermute | solution.py:322
  50.2 15.5 %collective-permute-start.14 = (f32[512,128]{1,0:T(8,128)S(1)}, f32[512,128]{1,0:T(8,128)S(1)}, u32[]{:S(2)}, u32[]{:S(2)}) collective-permute-start(f32[512,128]{1,0:T(8,128)S(1)} %get-tuple-element.90), channel_id=1, source_target_pairs={{0,8},{1,9},{2,10},{3,11},{4,12},{5,13},{6,14},{7,15},{8,16},{9,17... | collective-permute-start | bytes 786440 | tf_op jit(solution)/shard_map/ppermute | solution.py:322
  51.4 14.3 %collective-permute-start.15 = (f32[512,128]{1,0:T(8,128)S(1)}, f32[512,128]{1,0:T(8,128)S(1)}, u32[]{:S(2)}, u32[]{:S(2)}) collective-permute-start(f32[512,128]{1,0:T(8,128)S(1)} %get-tuple-element.91), channel_id=1, source_target_pairs={{0,24},{1,25},{2,26},{3,27},{4,28},{5,29},{6,30},{7,31},{8,0},{9,1... | collective-permute-start | bytes 786440 | tf_op jit(solution)/shard_map/ppermute | solution.py:322
  52.9 18.5 %collective-permute-start.16 = (f32[512,128]{1,0:T(8,128)S(1)}, f32[512,128]{1,0:T(8,128)S(1)}, u32[]{:S(2)}, u32[]{:S(2)}) collective-permute-start(f32[512,128]{1,0:T(8,128)S(1)} %get-tuple-element.92), channel_id=1, source_target_pairs={{0,9},{1,8},{2,11},{3,10},{4,13},{5,12},{6,15},{7,14},{8,17},{9,16... | collective-permute-start | bytes 786440 | tf_op jit(solution)/shard_map/ppermute | solution.py:322
  52.9 18.5 %collective-permute-start.17 = (f32[512,128]{1,0:T(8,128)S(1)}, f32[512,128]{1,0:T(8,128)S(1)}, u32[]{:S(2)}, u32[]{:S(2)}) collective-permute-start(f32[512,128]{1,0:T(8,128)S(1)} %get-tuple-element.93), channel_id=1, source_target_pairs={{0,25},{1,24},{2,27},{3,26},{4,29},{5,28},{6,31},{7,30},{8,1},{9,0... | collective-permute-start | bytes 786440 | tf_op jit(solution)/shard_map/ppermute | solution.py:322
  60.2 11.2 %collective-permute-start.18 = (f32[512,128]{1,0:T(8,128)S(1)}, f32[512,128]{1,0:T(8,128)S(1)}, u32[]{:S(2)}, u32[]{:S(2)}) collective-permute-start(f32[512,128]{1,0:T(8,128)S(1)} %get-tuple-element.95), channel_id=1, source_target_pairs={{0,1},{1,0},{2,3},{3,2},{4,5},{5,4},{6,7},{7,6},{8,9},{9,8},{10,11... | collective-permute-start | bytes 786440 | tf_op jit(solution)/shard_map/ppermute | solution.py:322
  74.0 9.1 %collective-permute-start.19 = (f32[512,128]{1,0:T(8,128)S(1)}, f32[512,128]{1,0:T(8,128)S(1)}, u32[]{:S(2)}, u32[]{:S(2)}) collective-permute-start(f32[512,128]{1,0:T(8,128)S(1)} %get-tuple-element.96), channel_id=1, source_target_pairs={{0,16},{1,17},{2,18},{3,19},{4,20},{5,21},{6,22},{7,23},{8,24},{9,... | collective-permute-start | bytes 786440 | tf_op jit(solution)/shard_map/ppermute | solution.py:322
  76.2 13.9 %collective-permute-start.20 = (f32[512,128]{1,0:T(8,128)S(1)}, f32[512,128]{1,0:T(8,128)S(1)}, u32[]{:S(2)}, u32[]{:S(2)}) collective-permute-start(f32[512,128]{1,0:T(8,128)S(1)} %get-tuple-element.97), channel_id=1, source_target_pairs={{0,17},{1,16},{2,19},{3,18},{4,21},{5,20},{6,23},{7,22},{8,25},{9,... | collective-permute-start | bytes 786440 | tf_op jit(solution)/shard_map/ppermute | solution.py:322
  77.6 17.5 %collective-permute-start.21 = (f32[512,128]{1,0:T(8,128)S(1)}, f32[512,128]{1,0:T(8,128)S(1)}, u32[]{:S(2)}, u32[]{:S(2)}) collective-permute-start(f32[512,128]{1,0:T(8,128)S(1)} %get-tuple-element.98), channel_id=1, source_target_pairs={{0,8},{1,9},{2,10},{3,11},{4,12},{5,13},{6,14},{7,15},{8,16},{9,17... | collective-permute-start | bytes 786440 | tf_op jit(solution)/shard_map/ppermute | solution.py:322
  78.9 16.3 %collective-permute-start.22 = (f32[512,128]{1,0:T(8,128)S(1)}, f32[512,128]{1,0:T(8,128)S(1)}, u32[]{:S(2)}, u32[]{:S(2)}) collective-permute-start(f32[512,128]{1,0:T(8,128)S(1)} %get-tuple-element.99), channel_id=1, source_target_pairs={{0,24},{1,25},{2,26},{3,27},{4,28},{5,29},{6,30},{7,31},{8,0},{9,1... | collective-permute-start | bytes 786440 | tf_op jit(solution)/shard_map/ppermute | solution.py:322
  80.4 20.4 %collective-permute-start.23 = (f32[512,128]{1,0:T(8,128)S(1)}, f32[512,128]{1,0:T(8,128)S(1)}, u32[]{:S(2)}, u32[]{:S(2)}) collective-permute-start(f32[512,128]{1,0:T(8,128)S(1)} %get-tuple-element.100), channel_id=1, source_target_pairs={{0,9},{1,8},{2,11},{3,10},{4,13},{5,12},{6,15},{7,14},{8,17},{9,16... | collective-permute-start | bytes 786440 | tf_op jit(solution)/shard_map/ppermute | solution.py:322
  83.1 17.7 %collective-permute-start.24 = (f32[512,128]{1,0:T(8,128)S(1)}, f32[512,128]{1,0:T(8,128)S(1)}, u32[]{:S(2)}, u32[]{:S(2)}) collective-permute-start(f32[512,128]{1,0:T(8,128)S(1)} %get-tuple-element.101), channel_id=1, source_target_pairs={{0,25},{1,24},{2,27},{3,26},{4,29},{5,28},{6,31},{7,30},{8,1},{9,0... | collective-permute-start | bytes 786440 | tf_op jit(solution)/shard_map/ppermute | solution.py:322
  90.1 10.6 %collective-permute-start.25 = (f32[512,128]{1,0:T(8,128)S(1)}, f32[512,128]{1,0:T(8,128)S(1)}, u32[]{:S(2)}, u32[]{:S(2)}) collective-permute-start(f32[512,128]{1,0:T(8,128)S(1)} %get-tuple-element.103), channel_id=1, source_target_pairs={{0,1},{1,0},{2,3},{3,2},{4,5},{5,4},{6,7},{7,6},{8,9},{9,8},{10,11... | collective-permute-start | bytes 786440 | tf_op jit(solution)/shard_map/ppermute | solution.py:322
  103.3 13.2 %collective-permute-start.27 = (f32[512,128]{1,0:T(8,128)S(1)}, f32[512,128]{1,0:T(8,128)S(1)}, u32[]{:S(2)}, u32[]{:S(2)}) collective-permute-start(f32[512,128]{1,0:T(8,128)S(1)} %get-tuple-element.111), channel_id=1, source_target_pairs={{0,32},{1,33},{2,34},{3,35},{4,36},{5,37},{6,38},{7,39},{8,40},{9,... | collective-permute-start | bytes 786440 | tf_op jit(solution)/shard_map/ppermute | solution.py:322
  103.8 15.4 %collective-permute-start.28 = (f32[512,128]{1,0:T(8,128)S(1)}, f32[512,128]{1,0:T(8,128)S(1)}, u32[]{:S(2)}, u32[]{:S(2)}) collective-permute-start(f32[512,128]{1,0:T(8,128)S(1)} %get-tuple-element.112), channel_id=1, source_target_pairs={{0,64},{1,65},{2,66},{3,67},{4,68},{5,69},{6,70},{7,71},{8,72},{9,... | collective-permute-start | bytes 786440 | tf_op jit(solution)/shard_map/ppermute | solution.py:322
  107.6 11.6 %collective-permute-start.29 = (f32[512,128]{1,0:T(8,128)S(1)}, f32[512,128]{1,0:T(8,128)S(1)}, u32[]{:S(2)}, u32[]{:S(2)}) collective-permute-start(f32[512,128]{1,0:T(8,128)S(1)} %get-tuple-element.113), channel_id=1, source_target_pairs={{0,96},{1,97},{2,98},{3,99},{4,100},{5,101},{6,102},{7,103},{8,104... | collective-permute-start | bytes 786440 | tf_op jit(solution)/shard_map/ppermute | solution.py:322
  (10 other events, 77.9 us)
